TPU v7x, 32 devices: a whole 2x2x4 slice. The times are simulated.
32 devices in a mesh: dp: 2 (over x), ctx: 4 (over y, core), exp: 4 (over z).
Axes of the slice: x: 2, y: 2, z: 4, core: 2. Of those that a mesh axis runs over, the one named last changes fastest.
Arguments:
- block_input: bfloat16 [8, 1024, 1024], P(('dp', 'exp'), 'ctx'), may hold values from -6 to 6
- positions: int32 [8, 1024], P(('dp', 'exp')), may hold values from 0 to 1023, as said below
- norm_gain: bfloat16 [1024], replicated, may hold values from 0.5 to 1.5
- query_weight: bfloat16 [1024, 1024], replicated, may hold values from -0.1875 to 0.1875
- key_weight: bfloat16 [1024, 512], replicated, may hold values from -0.1875 to 0.1875
- value_weight: bfloat16 [1024, 512], replicated, may hold values from -0.1875 to 0.1875
- output_weight: bfloat16 [1024, 1024], replicated, may hold values from -3 to 3
- mixer_gain: bfloat16 [1024], replicated, may hold values from 0.5 to 1.5
- router_weight: bfloat16 [1024, 32], replicated, may hold values from -0.09375 to 0.09375
- expert_gate: bfloat16 [32, 1024, 512], P(('ctx', 'exp')), may hold values from -0.1875 to 0.1875
- expert_up: bfloat16 [32, 1024, 512], P(('ctx', 'exp')), may hold values from -0.1875 to 0.1875
- expert_down: bfloat16 [32, 512, 1024], P(('ctx', 'exp')), may hold values from -1 to 1
- routes: int32 [8, 1024, 8], P(('dp', 'exp'), 'ctx'), may hold values from 0 to 31, all different within a row; in each aligned block of 256 rows (0 to 255, 256 to 511, ..., all dimensions but the last counted through in order) at most 128 rows name the same one
- cotangent: bfloat16 [8, 1024, 1024], P(('dp', 'exp'), 'ctx'), may hold values from -6 to 6
Outputs:
- out: bfloat16 [8, 1024, 1024], P(('dp', 'exp'), 'ctx')
- input_grad: bfloat16 [8, 1024, 1024], P(('dp', 'exp'), 'ctx')
- norm_gain_grad: float32 [1024], replicated
- query_grad: float32 [1024, 1024], replicated
- key_grad: float32 [1024, 512], replicated
- value_grad: float32 [1024, 512], replicated
- output_grad: float32 [1024, 1024], replicated
- mixer_gain_grad: float32 [1024], replicated
- router_grad: float32 [1024, 32], replicated
- gate_grad: float32 [32, 1024, 512], P(('ctx', 'exp'), 'dp')
- up_grad: float32 [32, 1024, 512], P(('ctx', 'exp'), 'dp')
- down_grad: float32 [32, 512, 1024], P(('ctx', 'exp'), 'dp')
Inputs may be any that keep to these rules, and one draw needn't show every extreme that they name: Within each sequence the positions are a permutation of 0 to 1023, made of runs of 128 consecutive rising positions, each run starting at a multiple of 128. `routes`: among the 256 tokens of one sequence block on one index of ctx, no expert is named more than 128 times.
All inputs are finite; a program needn't handle non-finite values.
Results may differ from a plain program's by a relative error of at most 0.018.
Values may be sent and summed in bfloat16 or wider, within the bound.
A program may use at most 192 MiB of HBM per device.

v0:
```python
import math

import jax
import jax.numpy as jnp
from jax import lax
from jax.sharding import PartitionSpec as P

HEADS = 16
KV_HEADS = 8
HD = 64


EPS = 1e-06
THETA = 10000.0
NEG = -1e30
HIGH = lax.Precision.HIGHEST


def rms_norm(values, gain):
    return values * lax.rsqrt(jnp.mean(values * values, axis=-1, keepdims=True) + EPS) * gain


def rotate(values, places):
    half = values.shape[-1] // 2
    freqs = THETA ** (-jnp.arange(half, dtype=jnp.float32) * 2.0 / values.shape[-1])
    angle = places.astype(jnp.float32)[:, None] * freqs[None, :]
    cosine = jnp.cos(angle)[:, None, :]
    sine = jnp.sin(angle)[:, None, :]
    first = values[..., :half]
    second = values[..., half:]
    return jnp.concatenate(
        [first * cosine - second * sine, second * cosine + first * sine], axis=-1
    )


def slot_tables(route, experts, capacity):
    count, top = route.shape
    flat = route.reshape(count * top)
    onehot = (flat[:, None] == jnp.arange(experts, dtype=jnp.int32)[None, :]).astype(jnp.int32)
    rank = jnp.sum((jnp.cumsum(onehot, axis=0) - 1) * onehot, axis=1)
    slot = flat * capacity + rank
    pair = (
        jnp.full((experts * capacity,), count * top, jnp.int32)
        .at[slot]
        .set(jnp.arange(count * top, dtype=jnp.int32))
    )
    return (slot, pair)


def send_rows(buffer):
    return lax.all_to_all(buffer, ("ctx", "exp"), split_axis=0, concat_axis=0, tiled=True)


def send_results(buffer):
    return lax.all_to_all(buffer, ("ctx", "exp"), split_axis=0, concat_axis=0, tiled=True)


def send_grads(buffer):
    return lax.all_to_all(buffer, ("ctx", "exp"), split_axis=0, concat_axis=0, tiled=True)


def send_returns(buffer):
    return lax.all_to_all(buffer, ("ctx", "exp"), split_axis=0, concat_axis=0, tiled=True)


def body(
    block_input,
    positions,
    norm_gain,
    query_weight,
    key_weight,
    value_weight,
    output_weight,
    mixer_gain,
    router_weight,
    expert_gate,
    expert_up,
    expert_down,
    routes,
    cotangent,
):
    f32 = jnp.float32
    bf16 = jnp.bfloat16
    rows = block_input.shape[1]
    width = block_input.shape[2]
    groups = HEADS // KV_HEADS
    experts = router_weight.shape[1]
    local_experts = expert_gate.shape[0]
    owners = experts // local_experts
    top = routes.shape[2]
    capacity = rows * top * 2 // experts
    places = positions[0]
    length = places.shape[0]
    own_places = lax.dynamic_slice_in_dim(places, lax.axis_index("ctx") * rows, rows)
    span = math.gcd(length, 512)
    blocks = length // span
    scale = HD ** (-0.5)
    inputs = block_input[0].astype(f32)
    gain_one = norm_gain.astype(f32)
    gain_two = mixer_gain.astype(f32)
    hidden_one = rms_norm(inputs, gain_one).astype(bf16)
    query_pre = jnp.dot(hidden_one, query_weight, preferred_element_type=f32).reshape(
        rows, HEADS, HD
    )
    key_pre = jnp.dot(hidden_one, key_weight, preferred_element_type=f32).reshape(
        rows, KV_HEADS, HD
    )
    value_low = jnp.dot(hidden_one, value_weight, preferred_element_type=f32).astype(bf16)
    query_low = rotate(query_pre, own_places).astype(bf16).reshape(rows, KV_HEADS, groups, HD)
    key_low = rotate(key_pre, own_places).astype(bf16).reshape(rows, KV_HEADS * HD)
    keys_all, values_all = (
        lax.all_gather(key_low, "ctx", axis=0, tiled=True),
        lax.all_gather(value_low, "ctx", axis=0, tiled=True),
    )
    key_blocks = keys_all.reshape(blocks, span, KV_HEADS, HD)
    value_blocks = values_all.reshape(blocks, span, KV_HEADS, HD)
    place_blocks = places.reshape(blocks, span)

    def scores_of(key_block, place_block):
        raw = jnp.einsum("qgrd,kgd->grqk", query_low, key_block, preferred_element_type=f32) * scale
        allowed = place_block[None, :] <= own_places[:, None]
        return (jnp.where(allowed[None, None], raw, NEG), allowed)

    def max_step(carry, item):
        top_score, total = carry
        scores, allowed = scores_of(item[0], item[1])
        new_top = jnp.maximum(top_score, jnp.max(scores, axis=-1))
        terms = jnp.where(allowed[None, None], jnp.exp(scores - new_top[..., None]), 0.0)
        total = total * jnp.exp(top_score - new_top) + jnp.sum(terms, axis=-1)
        return ((new_top, total), None)

    start = (jnp.full((KV_HEADS, groups, rows), NEG, f32), jnp.zeros((KV_HEADS, groups, rows), f32))
    (top_score, total), _ = lax.scan(max_step, start, (key_blocks, place_blocks))
    log_total = top_score + jnp.log(total)

    def value_step(accum, item):
        scores, _ = scores_of(item[0], item[2])
        probs_low = jnp.exp(scores - log_total[..., None]).astype(bf16)
        return (
            accum + jnp.einsum("grqk,kgd->qgrd", probs_low, item[1], preferred_element_type=f32),
            None,
        )

    attn_f32, _ = lax.scan(
        value_step,
        jnp.zeros((rows, KV_HEADS, groups, HD), f32),
        (key_blocks, value_blocks, place_blocks),
    )
    attn_low = attn_f32.reshape(rows, HEADS * HD).astype(bf16)
    mixed = inputs + jnp.dot(attn_low, output_weight, preferred_element_type=f32)
    hidden_two = rms_norm(mixed, gain_two).astype(bf16)
    logits = jnp.dot(hidden_two, router_weight, preferred_element_type=f32)
    route = routes[0]
    chosen = jnp.take_along_axis(logits, route, axis=1)
    gates = jax.nn.softmax(chosen, axis=-1)
    slot, pair = slot_tables(route, experts, capacity)
    source = jnp.where(pair < rows * top, pair // top, rows)
    padded = jnp.concatenate([hidden_two, jnp.zeros((1, width), bf16)], axis=0)
    outgoing = padded[source].reshape(owners, local_experts, capacity, width)
    arrived = send_rows(outgoing)
    gate_act = jnp.einsum("sjcd,jdf->sjcf", arrived, expert_gate, preferred_element_type=f32)
    up_act = jnp.einsum("sjcd,jdf->sjcf", arrived, expert_up, preferred_element_type=f32)
    product = (jax.nn.silu(gate_act) * up_act).astype(bf16)
    result = jnp.einsum("sjcf,jfd->sjcd", product, expert_down, preferred_element_type=f32).astype(
        bf16
    )
    returned = send_results(result).reshape(experts * capacity, width)
    picked = returned[slot].reshape(rows, top, width)
    output = (mixed + jnp.sum(gates[:, :, None] * picked.astype(f32), axis=1)).astype(bf16)
    grad_out = cotangent[0].astype(f32)
    gate_d = jnp.sum(picked.astype(f32) * grad_out[:, None, :], axis=2)
    chosen_d = gates * (gate_d - jnp.sum(gates * gate_d, axis=1, keepdims=True))
    onehot = (route[:, :, None] == jnp.arange(experts, dtype=jnp.int32)[None, None, :]).astype(f32)
    logits_d = jnp.sum(onehot * chosen_d[:, :, None], axis=1)
    slot_grads = (gates[:, :, None] * grad_out[:, None, :]).astype(bf16).reshape(rows * top, width)
    padded_grads = jnp.concatenate([slot_grads, jnp.zeros((1, width), bf16)], axis=0)
    grads_going = padded_grads[pair].reshape(owners, local_experts, capacity, width)
    grads_come = send_grads(grads_going)
    down_part = jnp.einsum("sjcf,sjcd->jfd", product, grads_come, preferred_element_type=f32)
    product_d = jnp.einsum("sjcd,jfd->sjcf", grads_come, expert_down, preferred_element_type=f32)
    _, silu_pull = jax.vjp(lambda g, u: jax.nn.silu(g) * u, gate_act, up_act)
    gate_act_d, up_act_d = silu_pull(product_d)
    gate_low = gate_act_d.astype(bf16)
    up_low = up_act_d.astype(bf16)
    gate_part = jnp.einsum("sjcd,sjcf->jdf", arrived, gate_low, preferred_element_type=f32)
    up_part = jnp.einsum("sjcd,sjcf->jdf", arrived, up_low, preferred_element_type=f32)
    arrived_d = jnp.einsum("sjcf,jdf->sjcd", gate_low, expert_gate, preferred_element_type=f32)
    arrived_d = (
        arrived_d + jnp.einsum("sjcf,jdf->sjcd", up_low, expert_up, preferred_element_type=f32)
    ).astype(bf16)
    returned_d = send_returns(arrived_d).reshape(experts * capacity, width)
    hidden_two_d = jnp.sum(returned_d[slot].reshape(rows, top, width).astype(f32), axis=1)
    hidden_two_d = hidden_two_d + jnp.dot(logits_d, router_weight.astype(f32).T, precision=HIGH)
    router_part = jnp.dot(hidden_two.astype(f32).T, logits_d, precision=HIGH)
    _, norm_two_pull = jax.vjp(rms_norm, mixed, gain_two)
    mixed_part, gain_two_part = norm_two_pull(hidden_two_d)
    mixed_d = grad_out + mixed_part
    mixed_low = mixed_d.astype(bf16)
    output_part = jnp.dot(attn_low.T, mixed_low, preferred_element_type=f32)
    attn_d = (
        jnp.dot(mixed_low, output_weight.T, preferred_element_type=f32)
        .astype(bf16)
        .reshape(rows, KV_HEADS, groups, HD)
    )
    delta = jnp.transpose(jnp.sum(attn_d.astype(f32) * attn_f32, axis=-1), (1, 2, 0))

    def grad_step(query_d, item):
        key_block, value_block, place_block = item
        scores, _ = scores_of(key_block, place_block)
        probs = jnp.exp(scores - log_total[..., None])
        probs_low = probs.astype(bf16)
        value_piece = jnp.einsum("grqk,qgrd->kgd", probs_low, attn_d, preferred_element_type=f32)
        probs_d = jnp.einsum("qgrd,kgd->grqk", attn_d, value_block, preferred_element_type=f32)
        scores_d = (probs * (probs_d - delta[..., None]) * scale).astype(bf16)
        query_d = query_d + jnp.einsum(
            "grqk,kgd->qgrd", scores_d, key_block, preferred_element_type=f32
        )
        key_piece = jnp.einsum("grqk,qgrd->kgd", scores_d, query_low, preferred_element_type=f32)
        return (
            query_d,
            (key_piece.reshape(span, KV_HEADS * HD), value_piece.reshape(span, KV_HEADS * HD)),
        )

    query_d, (keys_d, values_d) = lax.scan(
        grad_step,
        jnp.zeros((rows, KV_HEADS, groups, HD), f32),
        (key_blocks, value_blocks, place_blocks),
    )
    key_own, value_own = (
        lax.psum_scatter(
            keys_d.reshape(length, KV_HEADS * HD).astype(jnp.bfloat16),
            "ctx",
            scatter_dimension=0,
            tiled=True,
        ).astype(jnp.float32),
        lax.psum_scatter(
            values_d.reshape(length, KV_HEADS * HD).astype(jnp.bfloat16),
            "ctx",
            scatter_dimension=0,
            tiled=True,
        ).astype(jnp.float32),
    )
    _, query_pull = jax.vjp(lambda v: rotate(v, own_places), query_pre)
    query_back = (
        query_pull(query_d.reshape(rows, HEADS, HD))[0].reshape(rows, HEADS * HD).astype(bf16)
    )
    _, key_pull = jax.vjp(lambda v: rotate(v, own_places), key_pre)
    key_back = (
        key_pull(key_own.reshape(rows, KV_HEADS, HD))[0].reshape(rows, KV_HEADS * HD).astype(bf16)
    )
    value_back = value_own.astype(bf16)
    query_part = jnp.dot(hidden_one.T, query_back, preferred_element_type=f32)
    key_part = jnp.dot(hidden_one.T, key_back, preferred_element_type=f32)
    value_part = jnp.dot(hidden_one.T, value_back, preferred_element_type=f32)
    hidden_one_d = jnp.dot(query_back, query_weight.T, preferred_element_type=f32)
    hidden_one_d = hidden_one_d + jnp.dot(key_back, key_weight.T, preferred_element_type=f32)
    hidden_one_d = hidden_one_d + jnp.dot(value_back, value_weight.T, preferred_element_type=f32)
    _, norm_one_pull = jax.vjp(rms_norm, inputs, gain_one)
    input_part, gain_one_part = norm_one_pull(hidden_one_d)
    input_grad = (mixed_d + input_part).astype(bf16)
    shared = lax.psum(
        (gain_one_part, query_part, key_part, value_part, output_part, gain_two_part, router_part),
        ("dp", "ctx", "exp"),
    )
    owned = (
        lax.psum_scatter(
            gate_part.astype(jnp.bfloat16), "dp", scatter_dimension=1, tiled=True
        ).astype(jnp.float32),
        lax.psum_scatter(
            up_part.astype(jnp.bfloat16), "dp", scatter_dimension=1, tiled=True
        ).astype(jnp.float32),
        lax.psum_scatter(
            down_part.astype(jnp.bfloat16), "dp", scatter_dimension=1, tiled=True
        ).astype(jnp.float32),
    )
    return (
        output[None],
        input_grad[None],
        shared[0],
        shared[1],
        shared[2],
        shared[3],
        shared[4],
        shared[5],
        shared[6],
        owned[0],
        owned[1],
        owned[2],
    )


def solution(mesh):
    return jax.shard_map(
        body,
        mesh=mesh,
        in_specs=(
            P(("dp", "exp"), "ctx", None),
            P(("dp", "exp"), None),
            P(),
            P(),
            P(),
            P(),
            P(),
            P(),
            P(),
            P(("ctx", "exp"), None, None),
            P(("ctx", "exp"), None, None),
            P(("ctx", "exp"), None, None),
            P(("dp", "exp"), "ctx", None),
            P(("dp", "exp"), "ctx", None),
        ),
        out_specs=(
            P(("dp", "exp"), "ctx", None),
            P(("dp", "exp"), "ctx", None),
            P(),
            P(),
            P(),
            P(),
            P(),
            P(),
            P(),
            P(("ctx", "exp"), "dp", None),
            P(("ctx", "exp"), "dp", None),
            P(("ctx", "exp"), "dp", None),
        ),
        check_vma=False,
    )
```

profile of v0, /device:TPU:0, one launch (start us, length us, event | category | flops | bytes accessed | tf_op | source)
XLA Modules:
  0.0 1387.6 jit_solution(5943216417177701025)
XLA Ops:
  9.4 2.6 convolution_convert_fusion.1
  18.3 9.1 reduce-window.6
  29.7 4.0 copy.111
  33.8 8.4 scatter_custom_fusion
  42.2 2.4 fusion.107
  45.0 3.9 reshape.625
  48.9 3.3 copy.113
  52.2 2.6 reshape.546
  54.8 2.4 copy.114
  57.2 9.4 while.39
  57.3 2.4 fusion.208
  62.0 2.4 fusion.208
  66.6 10.4 while.40
  66.7 4.9 fusion.215
  71.8 5.2 fusion.215
  78.5 2.6 multiply_reduce_fusion.3
  82.9 18.3 %gather_fusion = bf16[4096,1024]{1,0:T(8,128)(2,1)} fusion(bf16[257,1024]{1,0:T(8,128)(2,1)S(1)} %concatenate.23, s32[4096]{0:T(1024)S(1)} %get-tuple-element.438), kind=kCustom, calls=%fused_computation | custom fusion | bytes 16793600 | tf_op jit(solution)/shard_map/gather | solution.py:159
  101.2 8.1 all-to-all-start
  112.0 16.8 %gather_fusion.4 = f32[2048]{0:T(1024)S(1)} fusion(f32[256,32]{0,1:T(8,128)S(1)} %fusion.144, s32[2048]{0:T(1024)S(1)} %reshape.594), kind=kCustom, calls=%fused_computation.4 | custom fusion | bytes 32768 | tf_op jit(solution)/shard_map/jit(take_along_axis)/gather | solution.py:154
  133.5 2.4 concatenate.24
  135.9 23.6 %gather_fusion.2 = bf16[4096,1024]{1,0:T(8,128)(2,1)} fusion(bf16[2049,1024]{1,0:T(8,128)(2,1)} %concatenate.24, s32[4096]{0:T(1024)S(1)} %get-tuple-element.437), kind=kCustom, calls=%fused_computation.2 | custom fusion | bytes 16793600 | tf_op jit(solution)/shard_map/gather | solution.py:177
  159.5 134.1 %all-to-all-done = bf16[16,2,128,1024]{3,2,1,0:T(8,128)(2,1)} async-done(((bf16[16,2,128,1024]{3,2,1,0:T(8,128)(2,1)}), bf16[16,2,128,1024]{3,2,1,0:T(8,128)(2,1)}, u32[]{:S(2)}, u32[]{:S(2)}) %all-to-all-start) | async-done | bytes 8388640 | tf_op jit(solution)/shard_map/all_to_all | solution.py:51
  293.6 4.8 all-to-all-start.2
  298.5 11.9 fusion.69
  310.4 10.1 fusion.71
  320.5 162.2 %all-to-all-done.2 = bf16[16,2,128,1024]{3,2,1,0:T(8,128)(2,1)} async-done(((bf16[16,2,128,1024]{3,2,1,0:T(8,128)(2,1)}), bf16[16,2,128,1024]{3,2,1,0:T(8,128)(2,1)}, u32[]{:S(2)}, u32[]{:S(2)}) %all-to-all-start.2) | async-done | bytes 8388640 | tf_op jit(solution)/shard_map/all_to_all | solution.py:59
  482.7 17.1 %fusion.59 = (bf16[16,2,128,512]{3,2,0,1:T(8,128)(2,1)}, bf16[16,2,128,512]{3,2,0,1:T(8,128)(2,1)}, bf16[16,2,128,512]{3,2,0,1:T(8,128)(2,1)}) fusion(f32[2,16,128,512]{3,2,1,0:T(8,128)} %fusion.71, f32[2,16,128,512]{3,2,1,0:T(8,128)} %fusion.69, bf16[2,512,1024]{2,1,0:T(8,128)(2,1)S(1)} %copy-done, bf16[16,2,128,1024]{3,2,1,0:T(8,128)(2,1)} %all-to-all-done.2), kind=kOutput, calls=%fused_computation.78 | convolution fusion | flops 4328521728 | bytes 39845888 | tf_op jit(solution)/shard_map/sjcd,jfd->sjcf/dot_general | solution.py:180
  499.8 9.2 convert_bitcast_fusion
  509.0 8.2 copy.124
  517.2 4.9 all-to-all-start.1
  522.1 10.4 fusion.81
  532.5 15.4 %fusion.58 = bf16[16,2,128,1024]{3,2,0,1:T(8,128)(2,1)} fusion(f32[2,16,128,1024]{3,2,1,0:T(8,128)} %fusion.81, bf16[16,2,128,512]{3,2,0,1:T(8,128)(2,1)} %get-tuple-element.424, bf16[2,1024,512]{2,1,0:T(8,128)(2,1)} %param.30), kind=kOutput, calls=%fused_computation.74 | convolution fusion | flops 4303355904 | bytes 31457280 | tf_op jit(solution)/shard_map/sjcf,jdf->sjcd/dot_general | solution.py:189
  547.9 8.2 copy.126
  556.1 150.2 %all-to-all-done.1 = bf16[16,2,128,1024]{3,2,1,0:T(8,128)(2,1)} async-done(((bf16[16,2,128,1024]{3,2,1,0:T(8,128)(2,1)}), bf16[16,2,128,1024]{3,2,1,0:T(8,128)(2,1)}, u32[]{:S(2)}, u32[]{:S(2)}) %all-to-all-start.1) | async-done | bytes 8388640 | tf_op jit(solution)/shard_map/all_to_all | solution.py:55
  706.3 4.8 all-to-all-start.3
  711.6 15.4 %gather_fusion.1 = bf16[2048,1024]{1,0:T(8,128)(2,1)} fusion(bf16[4096,1024]{1,0:T(8,128)(2,1)} %bitcast.29, s32[2048]{0:T(1024)S(1)} %broadcast_clamp_fusion), kind=kCustom, calls=%fused_computation.1 | custom fusion | bytes 8396800 | tf_op jit(solution)/shard_map/gather | solution.py:168
  727.0 6.2 fusion.54
  733.5 161.9 %all-to-all-done.3 = bf16[16,2,128,1024]{3,2,1,0:T(8,128)(2,1)} async-done(((bf16[16,2,128,1024]{3,2,1,0:T(8,128)(2,1)}), bf16[16,2,128,1024]{3,2,1,0:T(8,128)(2,1)}, u32[]{:S(2)}, u32[]{:S(2)}) %all-to-all-start.3) | async-done | bytes 8388640 | tf_op jit(solution)/shard_map/all_to_all | solution.py:63
  895.4 15.5 %gather_fusion.3 = bf16[2048,1024]{1,0:T(8,128)(2,1)} fusion(bf16[4096,1024]{1,0:T(8,128)(2,1)} %bitcast.41, s32[2048]{0:T(1024)S(1)} %broadcast_clamp_fusion), kind=kCustom, calls=%fused_computation.3 | custom fusion | bytes 8396800 | tf_op jit(solution)/shard_map/gather | solution.py:192
  910.9 5.7 convert_reduce_fusion
  924.5 43.8 %while.41 = (s32[]{:T(128)}, f32[256,8,2,64]{0,3,2,1:T(8,128)S(1)}, bf16[2,512,512]{2,1,0:T(8,128)(2,1)}, bf16[2,512,512]{2,1,0:T(8,128)(2,1)}, bf16[2,512,8,64]...) while((s32[]{:T(128)}, f32[256,8,2,64]{0,3,2,1:T(8,128)S(1)}, ...), condition=%wide.region_22.23_spmd.clone, body=%wide.region_21.22_spmd.clone.sunk | while | flops 1365901312 | bytes 70180056 | solution.py:224
  926.4 4.1 fusion.229
  930.6 5.3 fusion.227
  937.1 4.5 fusion.230
  948.1 4.1 fusion.229
  952.3 5.3 fusion.227
  958.9 4.5 fusion.230
  969.0 10.7 bitcast_convert_fusion
  979.9 10.6 bitcast_convert_fusion.1
  990.7 10.5 bitcast_convert_fusion.2
  1002.8 2.9 fusion.113
  1005.6 2.7 fusion.117
  1011.5 8.0 reduce-scatter.8.cloned.1.call-done
  1019.5 2.8 fusion.121
  1022.4 31.7 %reduce-scatter.14.cloned.1.call-done = bf16[2,256,1024]{2,1,0:T(8,128)(2,1)} async-done(((bf16[2,512,1024]{2,1,0:T(8,128)(2,1)}), bf16[2,256,1024]{2,1,0:T(8,128)(2,1)}) %reduce-scatter.14.cloned.1.call-update) | async-done | bytes 1048592 | tf_op jit(solution)/shard_map/reduce_scatter | solution.py:272
  1054.0 2.8 convert_element_type.236
  1056.8 31.8 %reduce-scatter.12.cloned.1.call-done = bf16[2,512,512]{2,1,0:T(8,128)(2,1)} async-done(((bf16[2,1024,512]{2,1,0:T(8,128)(2,1)}), bf16[2,512,512]{2,1,0:T(8,128)(2,1)}) %reduce-scatter.12.cloned.1.call-update) | async-done | bytes 1048592 | tf_op jit(solution)/shard_map/reduce_scatter | solution.py:269
  1088.7 2.8 convert_element_type.234
  1091.5 31.8 %reduce-scatter.10.cloned.1.call-done = bf16[2,512,512]{2,1,0:T(8,128)(2,1)} async-done(((bf16[2,1024,512]{2,1,0:T(8,128)(2,1)}), bf16[2,512,512]{2,1,0:T(8,128)(2,1)}) %reduce-scatter.10.cloned.1.call-update) | async-done | bytes 1048592 | tf_op jit(solution)/shard_map/reduce_scatter | solution.py:266
  1123.4 2.8 convert_element_type.232
  1126.2 2.3 fusion.145
  1132.2 41.0 %all-reduce.6 = (f32[1024]{0:T(1024)}, f32[1024]{0:T(1024)}) all-reduce(f32[1024]{0:T(1024)S(1)} %get-tuple-element.357, f32[1024]{0:T(1024)S(1)} %get-tuple-element.355), channel_id=1, replica_groups=mesh['dp'=2,'ctx'=4,'exp'=4] {'dp','ctx','exp'}, use_global_device_ids=true, to_apply=%region_27.28 | all-reduce | flops 2048 | bytes 16384 | tf_op jit(solution)/shard_map/psum | solution.py:261
  1174.3 195.9 %all-reduce.10.cloned.1.call-done = (f32[1024,1024]{1,0:T(8,128)}, f32[1024,512]{1,0:T(8,128)}, f32[1024,512]{1,0:T(8,128)}, f32[1024,1024]{1,0:T(8,128)}, f32[1024,32]{0,1:T(8,128)}) async-done(((f32[1024,1024]{1,0:T(8,128)}, f32[1024,512]{1,0:T(8,128)}, f32[1024,512]{1,0:T(8,128)}, f32[1024,1024]{1,0:T(8,128)}, f32[1024,32]{0,1:T(8,128)}), (f32[1024,1024]{1,0:T(8,128)}, f32[1024,512]{1,0:T(8,128)}, ...) | async-done | bytes 12714000 | tf_op jit(solution)/shard_map/psum | solution.py:261
  1370.2 5.1 copy.244
  (251 shorter events, 65.8 us)
Async XLA Ops:
  7.2 475.5 %copy-start = (bf16[2,512,1024]{2,1,0:T(8,128)(2,1)S(1)}, bf16[2,512,1024]{2,1,0:T(8,128)(2,1)}, u32[]{:S(2)}) copy-start(bf16[2,512,1024]{2,1,0:T(8,128)(2,1)} %param.31) | copy-start | bytes 6291460
  7.2 35.0 %copy-start.6 = (bf16[1,256,1024]{2,1,0:T(8,128)(2,1)S(1)}, bf16[1,256,1024]{2,1,0:T(8,128)(2,1)}, u32[]{:S(2)}) copy-start(bf16[1,256,1024]{2,1,0:T(8,128)(2,1)} %param.20) | copy-start | bytes 1572868
  7.2 21.6 %copy-start.53 = (s32[1,1024]{1,0:T(1,128)S(1)}, s32[1,1024]{1,0:T(1,128)}, u32[]{:S(2)}) copy-start(s32[1,1024]{1,0:T(1,128)} %param.21) | copy-start | bytes 12292
  7.2 10.8 copy-start.37
  7.2 22.2 %copy-start.54 = (bf16[1024]{0:T(1024)(128)(2,1)S(1)}, bf16[1024]{0:T(1024)(128)(2,1)}, u32[]{:S(2)}) copy-start(bf16[1024]{0:T(1024)(128)(2,1)} %param.27) | copy-start | bytes 6148
  7.2 37.7 %all-gather.3.cloned.1.call-start = ((), (), s32[]{:S(2)}) async-start(), calls=%async_computation.9 | async-start | bytes 1310720 | tf_op jit(solution)/shard_map/all_gather | solution.py:113
  8.7 9.4 copy-start.49
  8.7 36.0 %copy-start.41 = (f32[256]{0:T(256)}, f32[256]{0:T(256)S(1)}, u32[]{:S(2)}) copy-start(f32[256]{0:T(256)S(1)} %fusion.136) | copy-start | bytes 3076
  9.4 35.3 %copy-start.34 = (f32[1024]{0:T(1024)}, f32[1024]{0:T(1024)S(1)}, u32[]{:S(2)}) copy-start(f32[1024]{0:T(1024)S(1)} %convert_element_type.191) | copy-start | bytes 12292
  12.0 40.2 %all-gather.5.cloned.1.call-start = ((), (), s32[]{:S(2)}) async-start(), calls=%async_computation.10 | async-start | bytes 1310720 | tf_op jit(solution)/shard_map/all_gather | solution.py:112
  15.2 29.6 %copy-start.24 = (f32[256,32]{0,1:T(8,128)}, f32[256,32]{0,1:T(8,128)S(1)}, u32[]{:S(2)}) copy-start(f32[256,32]{0,1:T(8,128)S(1)} %get-tuple-element.439) | copy-start | bytes 98308
  15.2 29.6 %copy-start.26 = (f32[256,32]{0,1:T(8,128)}, f32[256,32]{0,1:T(8,128)S(1)}, u32[]{:S(2)}) copy-start(f32[256,32]{0,1:T(8,128)S(1)} %get-tuple-element.440) | copy-start | bytes 98308
  29.5 51.7 %copy-start.39 = (f32[1024]{0:T(1024)}, f32[1024]{0:T(1024)S(1)}, u32[]{:S(2)}) copy-start(f32[1024]{0:T(1024)S(1)} %convert_element_type.201) | copy-start | bytes 12292
  33.8 11.0 copy-start.43
  77.0 4.2 copy-start.3
  77.0 24.2 %copy-start.28 = (s32[256]{0:T(256)}, s32[256]{0:T(256)S(1)}, u32[]{:S(2)}) copy-start(s32[256]{0:T(256)S(1)} %get-tuple-element.789) | copy-start | bytes 3076
  77.0 24.2 %copy-start.30 = (s32[2,512]{1,0:T(2,128)}, s32[2,512]{1,0:T(2,128)S(1)}, u32[]{:S(2)}) copy-start(s32[2,512]{1,0:T(2,128)S(1)} %get-tuple-element.791) | copy-start | bytes 12292
  77.0 24.2 %copy-start.45 = (f32[8,2,256]{2,1,0:T(2,128)}, f32[8,2,256]{2,1,0:T(2,128)S(1)}, u32[]{:S(2)}) copy-start(f32[8,2,256]{2,1,0:T(2,128)S(1)} %get-tuple-element.796) | copy-start | bytes 49156
  81.1 20.1 %copy-start.51 = (f32[256]{0:T(256)}, f32[256]{0:T(256)S(1)}, u32[]{:S(2)}) copy-start(f32[256]{0:T(256)S(1)} %get-tuple-element.441) | copy-start | bytes 3076
  81.1 20.1 %copy-start.47 = (f32[256]{0:T(256)}, f32[256]{0:T(256)S(1)}, u32[]{:S(2)}) copy-start(f32[256]{0:T(256)S(1)} %fusion.137) | copy-start | bytes 3076
  101.2 9.6 copy-start.32
  101.2 192.4 %all-to-all-start = ((bf16[16,2,128,1024]{3,2,1,0:T(8,128)(2,1)}), bf16[16,2,128,1024]{3,2,1,0:T(8,128)(2,1)}, u32[]{:S(2)}, u32[]{:S(2)}) async-start(bf16[16,2,128,1024]{3,2,1,0:T(8,128)(2,1)} %bitcast.383), calls=%async_computation | async-start | bytes 16777216 | tf_op jit(solution)/shard_map/all_to_all | solution.py:51
  293.6 189.1 %all-to-all-start.2 = ((bf16[16,2,128,1024]{3,2,1,0:T(8,128)(2,1)}), bf16[16,2,128,1024]{3,2,1,0:T(8,128)(2,1)}, u32[]{:S(2)}, u32[]{:S(2)}) async-start(bf16[16,2,128,1024]{3,2,1,0:T(8,128)(2,1)} %bitcast.384), calls=%async_computation.2 | async-start | bytes 16777216 | tf_op jit(solution)/shard_map/all_to_all | solution.py:59
  298.4 11.9 copy-start.55
  517.2 4.9 copy-start.56
  517.2 189.1 %all-to-all-start.1 = ((bf16[16,2,128,1024]{3,2,1,0:T(8,128)(2,1)}), bf16[16,2,128,1024]{3,2,1,0:T(8,128)(2,1)}, u32[]{:S(2)}, u32[]{:S(2)}) async-start(bf16[16,2,128,1024]{3,2,1,0:T(8,128)(2,1)} %copy.124), calls=%async_computation.1 | async-start | bytes 16777216 | tf_op jit(solution)/shard_map/all_to_all | solution.py:55
  556.1 155.3 %copy-start.44 = (s32[2048,1]{0,1:T(1,128)S(1)}, s32[2048,1]{0,1:T(1,128)}, u32[]{:S(2)}) copy-start(s32[2048,1]{0,1:T(1,128)} %copy-done.43) | copy-start | bytes 24580
  706.3 189.1 %all-to-all-start.3 = ((bf16[16,2,128,1024]{3,2,1,0:T(8,128)(2,1)}), bf16[16,2,128,1024]{3,2,1,0:T(8,128)(2,1)}, u32[]{:S(2)}, u32[]{:S(2)}) async-start(bf16[16,2,128,1024]{3,2,1,0:T(8,128)(2,1)} %copy.126), calls=%async_computation.3 | async-start | bytes 16777216 | tf_op jit(solution)/shard_map/all_to_all | solution.py:63
  711.2 297.2 %reduce-scatter.6.cloned.1.call-start = ((), (), s32[]{:S(2)}) async-start(), calls=%async_computation.11 | async-start | bytes 1310720 | tf_op jit(solution)/shard_map/reduce_scatter | solution.py:230
  895.4 21.2 %copy-start.38 = (s32[1,256,8]{1,2,0:T(8,128)S(1)}, s32[1,256,8]{1,2,0:T(8,128)}, u32[]{:S(2)}) copy-start(s32[1,256,8]{1,2,0:T(8,128)} %param.32) | copy-start | bytes 24580
  895.4 21.3 %copy-start.33 = (bf16[1024,32]{0,1:T(8,128)(2,1)S(1)}, bf16[1024,32]{0,1:T(8,128)(2,1)}, u32[]{:S(2)}) copy-start(bf16[1024,32]{0,1:T(8,128)(2,1)} %param.28) | copy-start | bytes 196612
  895.4 21.3 %copy-start.40 = (f32[1024]{0:T(1024)S(1)}, f32[1024]{0:T(1024)}, u32[]{:S(2)}) copy-start(f32[1024]{0:T(1024)} %copy-done.39) | copy-start | bytes 12292
  895.4 21.3 %copy-start.48 = (f32[256]{0:T(256)S(1)}, f32[256]{0:T(256)}, u32[]{:S(2)}) copy-start(f32[256]{0:T(256)} %copy-done.47) | copy-start | bytes 3076
  910.9 8.1 copy-start.52
  910.9 8.1 copy-start.11
  910.9 8.1 copy-start.18
  910.9 8.1 copy-start.21
  910.9 10.3 copy-start.12
  916.6 7.9 copy-start.4
  916.6 7.9 copy-start.5
  916.6 7.9 copy-start.29
  916.6 7.9 copy-start.31
  916.6 7.9 copy-start.46
  937.1 4.5 copy-start.2
  958.8 4.5 copy-start.2
  968.4 51.1 %reduce-scatter.8.cloned.1.call-start = ((), (), s32[]{:S(2)}) async-start(), calls=%async_computation.12 | async-start | bytes 1310720 | tf_op jit(solution)/shard_map/reduce_scatter | solution.py:236
  969.0 85.1 %reduce-scatter.14.cloned.1.call-start = ((), (), s32[]{:S(2)}) async-start(), calls=%async_computation.15 | async-start | bytes 3145728 | tf_op jit(solution)/shard_map/reduce_scatter | solution.py:272
  979.7 109.0 %reduce-scatter.12.cloned.1.call-start = ((), (), s32[]{:S(2)}) async-start(), calls=%async_computation.14 | async-start | bytes 3145728 | tf_op jit(solution)/shard_map/reduce_scatter | solution.py:269
  990.6 10.9 copy-start.25
  990.6 10.9 copy-start.27
  990.6 11.2 copy-start.14
  990.6 12.2 copy-start.7
  990.6 12.2 copy-start.35
  990.6 12.2 copy-start.42
  990.6 132.7 %reduce-scatter.10.cloned.1.call-start = ((), (), s32[]{:S(2)}) async-start(), calls=%async_computation.13 | async-start | bytes 3145728 | tf_op jit(solution)/shard_map/reduce_scatter | solution.py:266
  1001.2 4.4 copy-start.9
  1001.2 368.9 %all-reduce.10.cloned.1.call-start = ((), (), s32[]{:S(2)}) async-start(), calls=%async_computation.16 | async-start | bytes 25427968 | tf_op jit(solution)/shard_map/psum | solution.py:261
  1022.4 107.9 %copy-start.23 = (bf16[256,512]{1,0:T(8,128)(2,1)S(1)}, bf16[256,512]{1,0:T(8,128)(2,1)}, u32[]{:S(2)}) copy-start(bf16[256,512]{1,0:T(8,128)(2,1)} %reduce-scatter.8.cloned.1.call-done) | copy-start | bytes 786436
  1056.8 116.4 %copy-start.50 = (f32[256]{0:T(256)S(1)}, f32[256]{0:T(256)}, u32[]{:S(2)}) copy-start(f32[256]{0:T(256)} %copy-done.49) | copy-start | bytes 3076
  1370.2 5.1 copy-start.20
  1370.2 6.4 copy-start.19
  1370.2 7.7 copy-start.17
  1370.2 10.4 copy-start.1
  1375.3 4.7 copy-start.36
  (7 other events, 18.8 us)
Sparse Core Ops, SparseCore 0:
  12.1 19.4 all-gather.2
  33.7 16.9 all-gather.4
  968.5 23.4 reduce-scatter.5
  994.6 24.8 reduce-scatter.7
  1022.2 31.8 reduce-scatter.13
  1056.8 31.8 reduce-scatter.11
  1091.5 31.8 reduce-scatter.9
  1132.1 238.0 all-reduce.9
where the time goes:
time: 1390 us
  waiting for transfers between devices  908 us (65%)
  matrix products  184 us (13%)
  local copies, waits for them, and re-layouts  167 us (12%)
  other arithmetic  47.1 us (3%)
  blocking collectives  41 us (3%)
  starting transfers between devices  23.5 us (2%)
  between operations  15.4 us (1%)
    psum x1, waiting for transfers between devices, body(): lax.psum((gain_one_part, query_part, key_part, value_part, output_part, g...  196 us
    all_to_all x1, waiting for transfers between devices, send_grads(): lax.all_to_all(buffer, ('ctx', 'exp'), split_axis=0, concat_axis=0, tiled...  162 us
    all_to_all x1, waiting for transfers between devices, send_returns(): lax.all_to_all(buffer, ('ctx', 'exp'), split_axis=0, concat_axis=0, tiled...  162 us
    all_to_all x1, waiting for transfers between devices, send_results(): lax.all_to_all(buffer, ('ctx', 'exp'), split_axis=0, concat_axis=0, tiled...  150 us
    all_to_all x1, waiting for transfers between devices, send_rows(): lax.all_to_all(buffer, ('ctx', 'exp'), split_axis=0, concat_axis=0, tiled...  134 us
    psum x1, blocking collectives, body(): lax.psum((gain_one_part, query_part, key_part, value_part, output_part, g...  41 us
    reduce_scatter x1, waiting for transfers between devices, body(): lax.psum_scatter(up_part.astype(jnp.bfloat16), 'dp', scatter_dimension=1,...  31.8 us
    reduce_scatter x1, waiting for transfers between devices, body(): lax.psum_scatter(gate_part.astype(jnp.bfloat16), 'dp', scatter_dimension=...  31.8 us
  transfers between devices with their start and end apart: 12, of which 9 were waited for; matrix products, arithmetic and copies ran while one was open for 16% of the time, Pallas kernels for 0%

commit v1 on v0

v1 whole, which is shorter than its diff:
```python
import math

import jax
import jax.numpy as jnp
from jax import lax
from jax.experimental import pallas as pl
from jax.experimental.pallas import tpu as pltpu
from jax.sharding import PartitionSpec as P

HEADS = 16
KV_HEADS = 8
HD = 64


EPS = 1e-06
THETA = 10000.0
NEG = -1e30
HIGH = lax.Precision.HIGHEST
GROUP = ("ctx", "exp")


def rms_norm(values, gain):
    return values * lax.rsqrt(jnp.mean(values * values, axis=-1, keepdims=True) + EPS) * gain


def rotate(values, places):
    half = values.shape[-1] // 2
    freqs = THETA ** (-jnp.arange(half, dtype=jnp.float32) * 2.0 / values.shape[-1])
    angle = places.astype(jnp.float32)[:, None] * freqs[None, :]
    cosine = jnp.cos(angle)[:, None, :]
    sine = jnp.sin(angle)[:, None, :]
    first = values[..., :half]
    second = values[..., half:]
    return jnp.concatenate(
        [first * cosine - second * sine, second * cosine + first * sine], axis=-1
    )


NN = (((1,), (0,)), ((), ()))
NT = (((1,), (1,)), ((), ()))
TN = (((0,), (0,)), ((), ()))


def mul(left, right, dims):
    return lax.dot_general(left, right, dims, preferred_element_type=jnp.float32)


def expert_kernel(
    blocks,
    capacity,
    hidden_ref,
    grads_ref,
    ranks_ref,
    gates_ref,
    gate_ref,
    up_ref,
    down_ref,
    out_ref,
    back_ref,
    dots_ref,
    gate_out,
    up_out,
    down_out,
    gate_acc,
    up_acc,
    down_acc,
):
    f32 = jnp.float32
    bf16 = jnp.bfloat16
    step = pl.program_id(0)
    local = gate_ref.shape[0]
    tokens = hidden_ref.shape[0] // blocks

    @pl.when(step == 0)
    def _():
        gate_acc[...] = jnp.zeros_like(gate_acc)
        up_acc[...] = jnp.zeros_like(up_acc)
        down_acc[...] = jnp.zeros_like(down_acc)

    lanes = lax.broadcasted_iota(jnp.int32, (capacity, tokens), 0).astype(f32)
    for j in range(local):
        picks = []
        shares = []
        rows = []
        grads = []
        for s in range(blocks):
            at = s * local + j
            pick = jnp.where(lanes == ranks_ref[0, at : at + 1, :], 1.0, 0.0)
            shares.append(
                jnp.sum(pick * gates_ref[0, at : at + 1, :], axis=1, keepdims=True)
            )
            picks.append(pick)
            low = pick.astype(bf16)
            span = slice(s * tokens, (s + 1) * tokens)
            rows.append(mul(low, hidden_ref[span, :], NN).astype(bf16))
            grads.append(mul(low, grads_ref[span, :], NN))
        row = jnp.concatenate(rows, axis=0)
        grad = jnp.concatenate(grads, axis=0)
        share = jnp.concatenate(shares, axis=0)
        gate_act = mul(row, gate_ref[j], NN)
        up_act = mul(row, up_ref[j], NN)
        sig = 1.0 / (1.0 + jnp.exp(-gate_act))
        silu = gate_act * sig
        product = (silu * up_act).astype(bf16)
        result = mul(product, down_ref[j], NN).astype(bf16).astype(f32)
        dots = jnp.sum(result * grad, axis=1, keepdims=True)
        result_d = (share * grad).astype(bf16)
        weighed = (share * result).astype(bf16)
        down_acc[j] += mul(product, result_d, TN)
        product_d = mul(result_d, down_ref[j], NT)
        gate_low = (product_d * up_act * (sig * (1.0 + gate_act * (1.0 - sig)))).astype(bf16)
        up_low = (product_d * silu).astype(bf16)
        gate_acc[j] += mul(row, gate_low, TN)
        up_acc[j] += mul(row, up_low, TN)
        row_d = (mul(gate_low, gate_ref[j], NT) + mul(up_low, up_ref[j], NT)).astype(bf16)
        for s in range(blocks):
            at = s * local + j
            part = slice(s * capacity, (s + 1) * capacity)
            span = slice(s * tokens, (s + 1) * tokens)
            dots_ref[0, at : at + 1, :] = jnp.sum(
                picks[s] * dots[part], axis=0, keepdims=True
            )
            low = picks[s].astype(bf16)
            out_piece = mul(low, weighed[part], TN)
            back_piece = mul(low, row_d[part], TN)
            if j > 0:
                out_piece = out_piece + out_ref[span, :].astype(f32)
                back_piece = back_piece + back_ref[span, :].astype(f32)
            out_ref[span, :] = out_piece.astype(bf16)
            back_ref[span, :] = back_piece.astype(bf16)

    @pl.when(step == pl.num_programs(0) - 1)
    def _():
        gate_out[...] = gate_acc[...].astype(bf16)
        up_out[...] = up_acc[...].astype(bf16)
        down_out[...] = down_acc[...].astype(bf16)


def run_experts(hidden, grads, marked, e_gate, e_up, e_down, capacity):
    owners, local, tokens = marked.shape
    width, inner = e_gate.shape[1:]
    blocks = 2
    steps = owners // blocks
    chosen = marked >= 0.0
    upper = (
        jnp.arange(tokens, dtype=jnp.int32)[:, None] <= jnp.arange(tokens, dtype=jnp.int32)[None, :]
    ).astype(jnp.bfloat16)
    counts = jnp.dot(
        chosen.astype(jnp.bfloat16).reshape(owners * local, tokens),
        upper,
        preferred_element_type=jnp.float32,
    ).reshape(owners, local, tokens)
    ranks = jnp.where(chosen, counts - 1.0, -1.0).reshape(steps, blocks * local, tokens)
    gates = jnp.maximum(marked, 0.0).reshape(steps, blocks * local, tokens)
    token_spec = pl.BlockSpec((blocks * tokens, width), lambda i: (i, 0))
    small_spec = pl.BlockSpec((1, blocks * local, tokens), lambda i: (i, 0, 0))
    whole = lambda shape: pl.BlockSpec(
        shape, lambda i: (0, 0, 0), pipeline_mode=pl.Buffered(1)
    )
    wide = (local, width, inner)
    tall = (local, inner, width)
    flops = 2 * owners * local * capacity * width * (9 * inner + 4 * tokens)
    return pl.pallas_call(
        lambda *refs: expert_kernel(blocks, capacity, *refs),
        grid=(steps,),
        in_specs=[
            token_spec,
            token_spec,
            small_spec,
            small_spec,
            whole(wide),
            whole(wide),
            whole(tall),
        ],
        out_specs=[token_spec, token_spec, small_spec, whole(wide), whole(wide), whole(tall)],
        out_shape=[
            jax.ShapeDtypeStruct(hidden.shape, jnp.bfloat16),
            jax.ShapeDtypeStruct(hidden.shape, jnp.bfloat16),
            jax.ShapeDtypeStruct(gates.shape, jnp.float32),
            jax.ShapeDtypeStruct(wide, jnp.bfloat16),
            jax.ShapeDtypeStruct(wide, jnp.bfloat16),
            jax.ShapeDtypeStruct(tall, jnp.bfloat16),
        ],
        scratch_shapes=[
            pltpu.VMEM(wide, jnp.float32),
            pltpu.VMEM(wide, jnp.float32),
            pltpu.VMEM(tall, jnp.float32),
        ],
        compiler_params=pltpu.CompilerParams(
            dimension_semantics=("arbitrary",), vmem_limit_bytes=56 * 1024 * 1024
        ),
        cost_estimate=pl.CostEstimate(
            flops=flops, bytes_accessed=8 * hidden.size + 12 * e_gate.size, transcendentals=0
        ),
    )(hidden, grads, ranks, gates, e_gate, e_up, e_down)


def swap(values):
    return lax.ppermute(values, "dp", [(0, 1), (1, 0)])


def dp_sum(values):
    if lax.axis_size("dp") == 2:
        return values.astype(jnp.float32) + swap(values).astype(jnp.float32)
    return lax.psum(values, "dp").astype(jnp.float32)


def dp_share(values):
    if lax.axis_size("dp") == 2:
        part = values.shape[1] // 2
        me = lax.axis_index("dp")
        other = lax.dynamic_slice_in_dim(values, (1 - me) * part, part, axis=1)
        return (lax.dynamic_slice_in_dim(values, me * part, part, axis=1), swap(other))
    total = lax.psum_scatter(values, "dp", scatter_dimension=1, tiled=True)
    return (total, jnp.zeros_like(total))


def spread(values, axes, count):
    copies = jnp.broadcast_to(values[None], (count,) + values.shape)
    return lax.all_to_all(copies, axes, split_axis=0, concat_axis=0, tiled=True)


def body(
    block_input,
    positions,
    norm_gain,
    query_weight,
    key_weight,
    value_weight,
    output_weight,
    mixer_gain,
    router_weight,
    expert_gate,
    expert_up,
    expert_down,
    routes,
    cotangent,
):
    f32 = jnp.float32
    bf16 = jnp.bfloat16
    rows = block_input.shape[1]
    width = block_input.shape[2]
    groups = HEADS // KV_HEADS
    experts = router_weight.shape[1]
    local_experts = expert_gate.shape[0]
    owners = experts // local_experts
    capacity = rows * routes.shape[2] * 2 // experts
    places = positions[0]
    length = places.shape[0]
    own_places = lax.dynamic_slice_in_dim(places, lax.axis_index("ctx") * rows, rows)
    span = math.gcd(length, 512)
    blocks = length // span
    scale = HD ** (-0.5)
    inputs = block_input[0].astype(f32)
    grad_out = cotangent[0].astype(f32)
    grads_all = lax.all_gather(cotangent[0], GROUP, axis=0, tiled=True)
    gain_one = norm_gain.astype(f32)
    gain_two = mixer_gain.astype(f32)
    hidden_one = rms_norm(inputs, gain_one).astype(bf16)
    query_pre = jnp.dot(hidden_one, query_weight, preferred_element_type=f32).reshape(
        rows, HEADS, HD
    )
    key_pre = jnp.dot(hidden_one, key_weight, preferred_element_type=f32).reshape(
        rows, KV_HEADS, HD
    )
    value_low = jnp.dot(hidden_one, value_weight, preferred_element_type=f32).astype(bf16)
    query_low = rotate(query_pre, own_places).astype(bf16).reshape(rows, KV_HEADS, groups, HD)
    key_low = rotate(key_pre, own_places).astype(bf16).reshape(rows, KV_HEADS * HD)
    ranks = length // rows
    pairs_all = spread(jnp.stack([key_low, value_low]), "ctx", ranks)
    keys_all = pairs_all[:, 0].reshape(length, KV_HEADS * HD)
    values_all = pairs_all[:, 1].reshape(length, KV_HEADS * HD)
    key_blocks = keys_all.reshape(blocks, span, KV_HEADS, HD)
    value_blocks = values_all.reshape(blocks, span, KV_HEADS, HD)
    place_blocks = places.reshape(blocks, span)

    def scores_of(key_block, place_block):
        raw = jnp.einsum("qgrd,kgd->grqk", query_low, key_block, preferred_element_type=f32) * scale
        allowed = place_block[None, :] <= own_places[:, None]
        return (jnp.where(allowed[None, None], raw, NEG), allowed)

    def max_step(carry, item):
        top_score, total = carry
        scores, allowed = scores_of(item[0], item[1])
        new_top = jnp.maximum(top_score, jnp.max(scores, axis=-1))
        terms = jnp.where(allowed[None, None], jnp.exp(scores - new_top[..., None]), 0.0)
        total = total * jnp.exp(top_score - new_top) + jnp.sum(terms, axis=-1)
        return ((new_top, total), None)

    start = (jnp.full((KV_HEADS, groups, rows), NEG, f32), jnp.zeros((KV_HEADS, groups, rows), f32))
    (top_score, total), _ = lax.scan(max_step, start, (key_blocks, place_blocks))
    log_total = top_score + jnp.log(total)

    def value_step(accum, item):
        scores, _ = scores_of(item[0], item[2])
        probs_low = jnp.exp(scores - log_total[..., None]).astype(bf16)
        return (
            accum + jnp.einsum("grqk,kgd->qgrd", probs_low, item[1], preferred_element_type=f32),
            None,
        )

    attn_f32, _ = lax.scan(
        value_step,
        jnp.zeros((rows, KV_HEADS, groups, HD), f32),
        (key_blocks, value_blocks, place_blocks),
    )
    attn_low = attn_f32.reshape(rows, HEADS * HD).astype(bf16)
    mixed = inputs + jnp.dot(attn_low, output_weight, preferred_element_type=f32)
    hidden_two = rms_norm(mixed, gain_two).astype(bf16)
    logits = jnp.dot(hidden_two, router_weight, preferred_element_type=f32)
    route = routes[0]
    onehot = jnp.any(
        route[:, :, None] == jnp.arange(experts, dtype=jnp.int32)[None, None, :], axis=1
    )
    top_logit = jnp.max(jnp.where(onehot, logits, -jnp.inf), axis=1, keepdims=True)
    powers = jnp.where(onehot, jnp.exp(jnp.minimum(logits - top_logit, 0.0)), 0.0)
    gates = powers / jnp.sum(powers, axis=1, keepdims=True)
    marked = lax.all_to_all(
        jnp.where(onehot, gates, -1.0).T.reshape(owners, local_experts, rows),
        GROUP,
        split_axis=0,
        concat_axis=0,
        tiled=True,
    )
    hidden_all = lax.all_gather(hidden_two, GROUP, axis=0, tiled=True)
    out_parts, back_parts, dots, gate_part, up_part, down_part = run_experts(
        hidden_all, grads_all, marked, expert_gate, expert_up, expert_down, capacity
    )
    gate_d = lax.all_to_all(
        dots.reshape(owners, local_experts, rows), GROUP, split_axis=0, concat_axis=0, tiled=True
    )
    gate_d = gate_d.reshape(experts, rows).T
    hidden_two_d = lax.psum_scatter(back_parts, GROUP, scatter_dimension=0, tiled=True).astype(f32)
    gate_share, up_share, down_share = dp_share(gate_part), dp_share(up_part), dp_share(down_part)
    out_parts, hidden_two_d = lax.optimization_barrier((out_parts, hidden_two_d))
    added = lax.psum_scatter(out_parts, GROUP, scatter_dimension=0, tiled=True).astype(f32)
    logits_d = gates * (gate_d - jnp.sum(gates * gate_d, axis=1, keepdims=True))
    hidden_two_d = hidden_two_d + jnp.dot(logits_d, router_weight.astype(f32).T, precision=HIGH)
    router_part = jnp.dot(logits_d.T, hidden_two.astype(f32), precision=HIGH)
    _, norm_two_pull = jax.vjp(rms_norm, mixed, gain_two)
    mixed_part, gain_two_part = norm_two_pull(hidden_two_d)
    mixed_d = grad_out + mixed_part
    mixed_low = mixed_d.astype(bf16)
    output_part = jnp.dot(attn_low.T, mixed_low, preferred_element_type=f32).astype(bf16)
    attn_d = (
        jnp.dot(mixed_low, output_weight.T, preferred_element_type=f32)
        .astype(bf16)
        .reshape(rows, KV_HEADS, groups, HD)
    )
    delta = jnp.transpose(jnp.sum(attn_d.astype(f32) * attn_f32, axis=-1), (1, 2, 0))

    def grad_step(query_d, item):
        key_block, value_block, place_block = item
        scores, _ = scores_of(key_block, place_block)
        probs = jnp.exp(scores - log_total[..., None])
        probs_low = probs.astype(bf16)
        value_piece = jnp.einsum("grqk,qgrd->kgd", probs_low, attn_d, preferred_element_type=f32)
        probs_d = jnp.einsum("qgrd,kgd->grqk", attn_d, value_block, preferred_element_type=f32)
        scores_d = (probs * (probs_d - delta[..., None]) * scale).astype(bf16)
        query_d = query_d + jnp.einsum(
            "grqk,kgd->qgrd", scores_d, key_block, preferred_element_type=f32
        )
        key_piece = jnp.einsum("grqk,qgrd->kgd", scores_d, query_low, preferred_element_type=f32)
        return (
            query_d,
            (key_piece.reshape(span, KV_HEADS * HD), value_piece.reshape(span, KV_HEADS * HD)),
        )

    query_d, (keys_d, values_d) = lax.scan(
        grad_step,
        jnp.zeros((rows, KV_HEADS, groups, HD), f32),
        (key_blocks, value_blocks, place_blocks),
    )
    going = jnp.stack([keys_d.reshape(length, -1), values_d.reshape(length, -1)]).astype(bf16)
    going = going.reshape(2, ranks, rows, KV_HEADS * HD).transpose(1, 0, 2, 3)
    going, gate_share, up_share, down_share = lax.optimization_barrier(
        (going, gate_share, up_share, down_share)
    )
    come = lax.all_to_all(going, "ctx", split_axis=0, concat_axis=0, tiled=True)
    come, output_part = lax.optimization_barrier((come, output_part))
    key_own, value_own = jnp.sum(come.astype(f32), axis=0)
    _, query_pull = jax.vjp(lambda v: rotate(v, own_places), query_pre)
    query_back = (
        query_pull(query_d.reshape(rows, HEADS, HD))[0].reshape(rows, HEADS * HD).astype(bf16)
    )
    _, key_pull = jax.vjp(lambda v: rotate(v, own_places), key_pre)
    key_back = (
        key_pull(key_own.reshape(rows, KV_HEADS, HD))[0].reshape(rows, KV_HEADS * HD).astype(bf16)
    )
    value_back = value_own.astype(bf16)
    back = jnp.concatenate([query_back, key_back, value_back], axis=1)
    late_part = jnp.dot(hidden_one.T, back, preferred_element_type=f32).astype(bf16)
    hidden_one_d = jnp.dot(query_back, query_weight.T, preferred_element_type=f32)
    hidden_one_d = hidden_one_d + jnp.dot(key_back, key_weight.T, preferred_element_type=f32)
    hidden_one_d = hidden_one_d + jnp.dot(value_back, value_weight.T, preferred_element_type=f32)
    _, norm_one_pull = jax.vjp(rms_norm, inputs, gain_one)
    input_part, gain_one_part = norm_one_pull(hidden_one_d)
    input_grad = (mixed_d + input_part).astype(bf16)
    output_part, added = lax.optimization_barrier((output_part, added))
    output = (mixed + added).astype(bf16)
    output_sum = lax.psum_scatter(output_part, GROUP, scatter_dimension=0, tiled=True)
    late_part, output_sum = lax.optimization_barrier((late_part, output_sum))
    late_sum = lax.psum_scatter(late_part, GROUP, scatter_dimension=0, tiled=True)
    output_sum = dp_sum(output_sum).astype(bf16)
    output_total = lax.all_gather(output_sum, GROUP, axis=0, tiled=True).astype(f32)
    late_sum = dp_sum(late_sum).astype(bf16)
    late_total = lax.all_gather(late_sum, GROUP, axis=0, tiled=True).astype(f32)
    few = -(-(experts + 2) // owners)
    small = jnp.concatenate(
        [
            router_part,
            gain_one_part[None],
            gain_two_part[None],
            jnp.zeros((few * owners - experts - 2, width), f32),
        ],
        axis=0,
    ).reshape(owners, few, width)
    small = lax.all_to_all(small, GROUP, split_axis=0, concat_axis=0, tiled=True)
    small = dp_sum(jnp.sum(small, axis=0))
    small = spread(small, GROUP, owners).reshape(few * owners, width)
    wide = query_back.shape[1]
    kv_wide = key_back.shape[1]
    shared = (
        small[experts],
        late_total[:, :wide],
        late_total[:, wide : wide + kv_wide],
        late_total[:, wide + kv_wide :],
        output_total,
        small[experts + 1],
        small[:experts].T,
    )
    owned = tuple(
        own.astype(f32) + other.astype(f32) for own, other in (gate_share, up_share, down_share)
    )
    return (
        output[None],
        input_grad[None],
        shared[0],
        shared[1],
        shared[2],
        shared[3],
        shared[4],
        shared[5],
        shared[6],
        owned[0],
        owned[1],
        owned[2],
    )


def solution(mesh):
    return jax.shard_map(
        body,
        mesh=mesh,
        in_specs=(
            P(("dp", "exp"), "ctx", None),
            P(("dp", "exp"), None),
            P(),
            P(),
            P(),
            P(),
            P(),
            P(),
            P(),
            P(("ctx", "exp"), None, None),
            P(("ctx", "exp"), None, None),
            P(("ctx", "exp"), None, None),
            P(("dp", "exp"), "ctx", None),
            P(("dp", "exp"), "ctx", None),
        ),
        out_specs=(
            P(("dp", "exp"), "ctx", None),
            P(("dp", "exp"), "ctx", None),
            P(),
            P(),
            P(),
            P(),
            P(),
            P(),
            P(),
            P(("ctx", "exp"), "dp", None),
            P(("ctx", "exp"), "dp", None),
            P(("ctx", "exp"), "dp", None),
        ),
        check_vma=False,
    )
```

time: 1390 us -> 730 us (0.53)
  waiting for transfers between devices: 908 us -> 397 us
  matrix products: 184 us -> 81 us
  local copies, waits for them, and re-layouts: 167 us -> 72 us
  Pallas kernels: 0 us -> 67.7 us
  blocking collectives: 41 us -> 12.5 us
    all_to_all x4 -> x5, waiting for transfers between devices: 608 us -> 62.6 us  [the longest x2 29.5 us: spread(): return lax.all_to_all(copies, axes, split_axis=0, concat_axis=0, tiled=True)]
    psum x1 -> x0, waiting for transfers between devices: 196 us -> none  [body(): lax.psum((gain_one_part, query_part, key_part, value_part, output_part, g...]
    reduce_scatter x5 -> x4, waiting for transfers between devices: 103 us -> 222 us  [the longest x1 103 us: body(): lax.psum_scatter(back_parts, GROUP, scatter_dimension=0, tiled=True)]
    dot_general x14 -> x4, matrix products: 117 us -> 6.98 us  [the longest x1 4.44 us: body(): jnp.dot(hidden_one.T, back, preferred_element_type=f32).astype(bf16)]
    all_gather x2 -> x4, waiting for transfers between devices: 0.02 us -> 101 us  [the longest x1 60.8 us: body(): hidden_all = lax.all_gather(hidden_two, GROUP, axis=0, tiled=True)]
    gather x8 -> x0, local copies, waits for them, and re-layouts: 89.9 us -> none  [the longest x1 23.6 us: body(): padded_grads[pair].reshape(owners, local_experts, capacity, width)]
    pallas_call x0 -> x1, Pallas kernels: none -> 67.7 us  [run_experts(): pl.pallas_call(lambda *refs: expert_kernel(blocks, capacity, *refs), grid...]
    psum x1 -> x0, blocking collectives: 41 us -> none  [body(): lax.psum((gain_one_part, query_part, key_part, value_part, output_part, g...]
  transfers between devices with their start and end apart: 12 -> 19, of which waited for: 9 -> 12; matrix products, arithmetic and copies ran while one was open for 16% -> 25% of each run, Pallas kernels for 0% -> 0%
where the time goes in v1:
time: 730 us; the launch traced here: 726 us
  waiting for transfers between devices  397 us (54%)
  matrix products  81 us (11%)
  local copies, waits for them, and re-layouts  72 us (10%)
  Pallas kernels  67.7 us (9%)
  other arithmetic  49.4 us (7%)
  starting transfers between devices  30.7 us (4%)
  between operations  15.2 us (2%)
  blocking collectives  12.5 us (2%)
    reduce_scatter x1, waiting for transfers between devices, body(): lax.psum_scatter(back_parts, GROUP, scatter_dimension=0, tiled=True)  103 us
    reduce_scatter x1, waiting for transfers between devices, body(): lax.psum_scatter(late_part, GROUP, scatter_dimension=0, tiled=True)  69.3 us
    pallas_call x1, Pallas kernels, run_experts(): pl.pallas_call(lambda *refs: expert_kernel(blocks, capacity, *refs), grid...  67.7 us
    all_gather x1, waiting for transfers between devices, body(): hidden_all = lax.all_gather(hidden_two, GROUP, axis=0, tiled=True)  60.8 us
    reduce_scatter x1, waiting for transfers between devices, body(): lax.psum_scatter(output_part, GROUP, scatter_dimension=0, tiled=True)  49.5 us
    all_gather x1, waiting for transfers between devices, body(): late_total = lax.all_gather(late_sum, GROUP, axis=0, tiled=True).astype(f32)  40.2 us
    all_to_all x2, waiting for transfers between devices, spread(): return lax.all_to_all(copies, axes, split_axis=0, concat_axis=0, tiled=True)  29.5 us
    all_to_all x1, waiting for transfers between devices, body(): come = lax.all_to_all(going, 'ctx', split_axis=0, concat_axis=0, tiled=True)  27.9 us
  transfers between devices with their start and end apart: 19, of which 12 were waited for; matrix products, arithmetic and copies ran while one was open for 25% of the time, Pallas kernels for 0%

profile of v1, /device:TPU:0, one launch (start us, length us, event | category | flops | bytes accessed | tf_op | source)
XLA Modules:
  0.0 725.7 jit_solution(3955610185476494354)
XLA Ops:
  9.3 2.3 copy.91
  20.6 4.6 all-to-all-start
  25.8 4.0 copy.96
  31.0 2.4 fusion.84
  33.6 21.8 %all-to-all-done = bf16[4,2,256,512]{2,3,1,0:T(8,128)(2,1)} async-done(((bf16[4,2,256,512]{2,3,1,0:T(8,128)(2,1)}), bf16[4,2,256,512]{2,3,1,0:T(8,128)(2,1)}, u32[]{:S(2)}, u32[]{:S(2)}) %all-to-all-start) | async-done | bytes 2097184 | tf_op jit(solution)/shard_map/all_to_all | solution.py:220
  55.5 2.6 fusion.110
  59.9 3.5 reshape_reshape_squeeze.7
  63.4 2.5 copy.99
  65.8 3.0 copy.94
  68.8 3.5 reshape_reshape_squeeze.6
  72.3 2.4 copy.98
  74.7 21.1 %while.39 = (s32[]{:T(128)}, f32[8,2,256]{2,1,0:T(2,128)S(1)}, f32[8,2,256]{2,1,0:T(2,128)S(1)}, s32[2,512]{1,0:T(2,128)S(1)}, s32[256]{0:T(256)S(1)}, /*index=5...) while((s32[]{:T(128)}, f32[8,2,256]{2,1,0:T(2,128)S(1)}, ...), condition=%wide.region_4.5_spmd.clone, body=%wide.region_1.4_spmd.clone.sunk | while | flops 285364224 | bytes 18439788 | solution.py:291
  74.8 5.8 fusion.164
  80.7 4.6 select_reduce_fusion.3
  85.5 5.7 fusion.164
  91.2 4.5 select_reduce_fusion.3
  95.8 10.4 %while.40 = (s32[]{:T(128)}, f32[256,8,2,64]{0,3,2,1:T(8,128)}, bf16[2,512,8,64]{1,3,2,0:T(8,128)(2,1)}, s32[2,512]{1,0:T(2,128)S(1)}, s32[256]{0:T(256)S(1)}, /...) while((s32[]{:T(128)}, f32[256,8,2,64]{0,3,2,1:T(8,128)}, ...), condition=%wide.region_6.7_spmd.clone, body=%wide.region_5.6_spmd.clone.sunk | while | flops 545914880 | bytes 3956851 | solution.py:302
  96.0 4.9 fusion.171
  101.0 5.2 fusion.171
  111.9 12.5 %all_to_all.30 = f32[16,2,256]{2,1,0:T(2,128)S(1)} all-to-all(f32[16,2,256]{2,1,0:T(2,128)S(1)} %reshape.319), channel_id=1, replica_groups=mesh['dp'=2,'ctx'=4,'exp'=4] {'ctx','exp'}, dimensions={0} | all-to-all | bytes 65536 | tf_op jit(solution)/shard_map/all_to_all | solution.py:318
  125.9 60.8 %all-gather.6.cloned.1.call-done.refs_0_ = bf16[4096,1024]{1,0:T(8,128)(2,1)} async-done(((bf16[256,1024]{1,0:T(8,128)(2,1)}), bf16[4096,1024]{1,0:T(8,128)(2,1)}) %all-gather.6.cloned.1.call-update) | async-done | bytes 8388624 | tf_op jit(solution)/shard_map/all_gather | solution.py:325
  186.7 67.7 %shard_map.229 = (bf16[4096,1024]{1,0:T(8,128)(2,1)}, bf16[4096,1024]{1,0:T(8,128)(2,1)}, f32[8,4,256]{2,1,0:T(4,128)}, bf16[2,1024,512]{2,1,0:T(8,128)(2,1)}, b...) custom-call(bf16[4096,1024]{1,0:T(8,128)(2,1)} %all-gather.6.cloned.1.call-done.refs_0_, ...), custom_call_target="tpu_custom_call" | custom-call | flops 47244640256 | bytes 46137344 | tf_op jit(solution)/shard_map/pallas_call | solution.py:163
  254.4 103.0 %reduce-scatter.5.cloned.1.call-done = bf16[256,1024]{1,0:T(8,128)(2,1)} async-done(((bf16[4096,1024]{1,0:T(8,128)(2,1)}), bf16[256,1024]{1,0:T(8,128)(2,1)}) %reduce-scatter.5.cloned.1.call-update) | async-done | bytes 524304 | tf_op jit(solution)/shard_map/reduce_scatter | solution.py:333
  357.4 2.1 convert_element_type.181
  360.9 4.7 all-to-all-start.2
  365.6 3.4 constant_dynamic-slice_fusion.7
  375.7 3.3 multiply_reduce_fusion
  384.9 51.0 %while.41 = (s32[]{:T(128)}, f32[256,8,2,64]{0,3,2,1:T(8,128)}, bf16[2,512,512]{2,1,0:T(8,128)(2,1)}, bf16[2,512,512]{2,1,0:T(8,128)(2,1)}, bf16[2,512,8,64]{1,3...) while((s32[]{:T(128)}, f32[256,8,2,64]{0,3,2,1:T(8,128)}, ...), condition=%wide.region_16.17_spmd.clone, body=%wide.region_15.16_spmd.clone.sunk | while | flops 1365901312 | bytes 116318528 | solution.py:369
  385.0 2.4 fusion.182
  387.6 4.4 fusion.183
  395.6 6.4 fusion.185
  402.0 2.1 copy.151
  404.2 2.1 constant_dynamic-update-slice_fusion.3
  406.3 3.0 fusion.184
  410.4 2.4 fusion.182
  413.0 4.4 fusion.183
  421.1 6.5 fusion.185
  427.6 2.2 copy.151
  429.8 2.1 constant_dynamic-update-slice_fusion.3
  431.9 3.0 fusion.184
  441.3 4.5 all-to-all-start.3
  445.8 2.0 convolution_convert_fusion.1
  447.9 27.9 %all-to-all-done.3 = bf16[4,2,256,512]{3,2,1,0:T(8,128)(2,1)} async-done(((bf16[4,2,256,512]{3,2,1,0:T(8,128)(2,1)}), bf16[4,2,256,512]{3,2,1,0:T(8,128)(2,1)}, u32[]{:S(2)}, u32[]{:S(2)}) %all-to-all-start.3) | async-done | bytes 2097184 | tf_op jit(solution)/shard_map/all_to_all | solution.py:379
  475.7 2.1 convert_element_type.186
  478.5 2.2 convert_reduce_fusion
  481.6 2.0 copy.111
  485.7 4.4 convolution_convert_fusion
  490.1 49.5 %reduce-scatter.9.cloned.1.call-done = bf16[64,1024]{1,0:T(8,128)(2,1)} async-done(((bf16[1024,1024]{1,0:T(8,128)(2,1)}), bf16[64,1024]{1,0:T(8,128)(2,1)}) %reduce-scatter.9.cloned.1.call-update) | async-done | bytes 131088 | tf_op jit(solution)/shard_map/reduce_scatter | solution.py:401
  541.2 3.7 collective-permute-done.5
  546.6 69.3 %reduce-scatter.11.cloned.1.call-done = bf16[64,2048]{1,0:T(8,128)(2,1)} async-done(((bf16[1024,2048]{1,0:T(8,128)(2,1)}), bf16[64,2048]{1,0:T(8,128)(2,1)}) %reduce-scatter.11.cloned.1.call-update) | async-done | bytes 262160 | tf_op jit(solution)/shard_map/reduce_scatter | solution.py:403
  617.3 5.1 collective-permute-done.4
  624.7 2.6 fusion.114
  630.3 4.2 all-to-all-start.4
  634.5 4.8 convert_add_fusion.1
  639.3 5.2 all-to-all-done.4
  646.2 3.3 convert_add_fusion
  650.2 3.5 all-to-all-start.5
  653.8 2.3 fusion.76
  656.1 7.7 %all-to-all-done.5 = f32[16,3,1024]{2,1,0:T(4,128)S(1)} async-done(((f32[16,3,1024]{2,1,0:T(4,128)}), f32[16,3,1024]{2,1,0:T(4,128)S(1)}, u32[]{:S(2)}, u32[]{:S(2)}) %all-to-all-start.5) | async-done | bytes 196640 | tf_op jit(solution)/shard_map/all_to_all | solution.py:220
  665.2 2.2 fusion.75
  667.3 4.1 convert_element_type.203
  671.5 40.2 %all-gather.8.cloned.1.call-done = bf16[1024,2048]{1,0:T(8,128)(2,1)} async-done(((bf16[64,2048]{1,0:T(8,128)(2,1)}), bf16[1024,2048]{1,0:T(8,128)(2,1)}) %all-gather.8.cloned.1.call-update) | async-done | bytes 4194320 | tf_op jit(solution)/shard_map/all_gather | solution.py:407
  711.7 4.3 fusion.109
  716.0 2.5 slice.55
  (233 shorter events, 68.5 us)
Async XLA Ops:
  7.2 100.4 %copy-start = (bf16[1024,1024]{1,0:T(8,128)(2,1)S(1)}, bf16[1024,1024]{1,0:T(8,128)(2,1)}, u32[]{:S(2)}) copy-start(bf16[1024,1024]{1,0:T(8,128)(2,1)} %param.26) | copy-start | bytes 6291460
  7.2 8.1 %copy-start.14 = (bf16[1,256,1024]{2,1,0:T(8,128)(2,1)S(1)}, bf16[1,256,1024]{2,1,0:T(8,128)(2,1)}, u32[]{:S(2)}) copy-start(bf16[1,256,1024]{2,1,0:T(8,128)(2,1)} %param.20) | copy-start | bytes 1572868
  7.2 118.7 %all-gather.12.cloned.1.call-start = ((), (), s32[]{:S(2)}) async-start(), calls=%async_computation.17 | async-start | bytes 8912896 | tf_op jit(solution)/shard_map/all_gather | solution.py:256
  9.3 21.6 %copy-start.30 = (f32[1024]{0:T(1024)}, f32[1024]{0:T(1024)S(1)}, u32[]{:S(2)}) copy-start(f32[1024]{0:T(1024)S(1)} %convert_element_type.169) | copy-start | bytes 12292
  12.8 6.3 copy-start.38
  12.9 18.1 %copy-start.40 = (f32[256]{0:T(256)}, f32[256]{0:T(256)S(1)}, u32[]{:S(2)}) copy-start(f32[256]{0:T(256)S(1)} %fusion.103) | copy-start | bytes 3076
  13.1 20.3 %copy-start.25 = (f32[256,32]{0,1:T(8,128)}, f32[256,32]{0,1:T(8,128)S(1)}, u32[]{:S(2)}) copy-start(f32[256,32]{0,1:T(8,128)S(1)} %get-tuple-element.477) | copy-start | bytes 98308
  13.1 20.3 %copy-start.27 = (f32[256,32]{0,1:T(8,128)}, f32[256,32]{0,1:T(8,128)S(1)}, u32[]{:S(2)}) copy-start(f32[256,32]{0,1:T(8,128)S(1)} %get-tuple-element.478) | copy-start | bytes 98308
  20.6 9.7 %copy-start.43 = (s32[1,1024]{1,0:T(1,128)S(1)}, s32[1,1024]{1,0:T(1,128)}, u32[]{:S(2)}) copy-start(s32[1,1024]{1,0:T(1,128)} %param.21) | copy-start | bytes 12292
  20.6 10.3 %copy-start.44 = (bf16[1024]{0:T(1024)(128)(2,1)S(1)}, bf16[1024]{0:T(1024)(128)(2,1)}, u32[]{:S(2)}) copy-start(bf16[1024]{0:T(1024)(128)(2,1)} %param.27) | copy-start | bytes 6148
  20.6 34.9 %all-to-all-start = ((bf16[4,2,256,512]{2,3,1,0:T(8,128)(2,1)}), bf16[4,2,256,512]{2,3,1,0:T(8,128)(2,1)}, u32[]{:S(2)}, u32[]{:S(2)}) async-start(bf16[4,2,256,512]{2,3,1,0:T(8,128)(2,1)} %broadcast_in_dim.83), calls=%async_computation | async-start | bytes 4194304 | tf_op jit(solution)/shard_map/all_to_all | solution.py:220
  25.2 161.5 %all-gather.6.cloned.1.call-start = ((), (), s32[]{:S(2)}) async-start(), calls=%async_computation.10 | async-start | bytes 8912896 | tf_op jit(solution)/shard_map/all_gather | solution.py:325
  106.2 4.2 copy-start.42
  106.2 4.2 copy-start.29
  110.3 247.1 %reduce-scatter.5.cloned.1.call-start = ((), (), s32[]{:S(2)}) async-start(), calls=%async_computation.11 | async-start | bytes 8912896 | tf_op jit(solution)/shard_map/reduce_scatter | solution.py:333
  111.8 263.9 %copy-start.33 = (f32[256]{0:T(256)}, f32[256]{0:T(256)S(1)}, u32[]{:S(2)}) copy-start(f32[256]{0:T(256)S(1)} %fusion.98) | copy-start | bytes 3076
  254.4 221.4 %reduce-scatter.7.cloned.1.call-start = ((), (), s32[]{:S(2)}) async-start(), calls=%async_computation.12 | async-start | bytes 8912896 | tf_op jit(solution)/shard_map/reduce_scatter | solution.py:336
  360.9 14.7 %all-to-all-start.2 = ((f32[16,2,256]{2,1,0:T(2,128)}), f32[16,2,256]{2,1,0:T(2,128)S(1)}, u32[]{:S(2)}, u32[]{:S(2)}) async-start(f32[16,2,256]{2,1,0:T(2,128)} %reshape.322), calls=%async_computation.3 | async-start | bytes 65536 | tf_op jit(solution)/shard_map/all_to_all | solution.py:329
  365.6 5.0 copy-start.21
  365.6 6.9 copy-start.20
  369.0 68.7 %collective-permute-start = (bf16[2,512,512]{2,1,0:T(8,128)(2,1)}, bf16[2,512,512]{2,1,0:T(8,128)(2,1)}, u32[]{:S(2)}, u32[]{:S(2)}) collective-permute-start(bf16[2,512,512]{2,1,0:T(8,128)(2,1)} %get-tuple-element.463), channel_id=1, source_target_pairs={{0,16},{16,0},{1,17},{17,1},{2,18},{18,2},{3,19},{19,3},{4,20},{20... | collective-permute-start | bytes 3145736 | tf_op jit(solution)/shard_map/ppermute | solution.py:199
  372.1 6.9 copy-start.22
  372.1 65.6 %collective-permute-start.1 = (bf16[2,512,512]{2,1,0:T(8,128)(2,1)}, bf16[2,512,512]{2,1,0:T(8,128)(2,1)}, u32[]{:S(2)}, u32[]{:S(2)}) collective-permute-start(bf16[2,512,512]{2,1,0:T(8,128)(2,1)} %get-tuple-element.461), channel_id=1, source_target_pairs={{0,16},{16,0},{1,17},{17,1},{2,18},{18,2},{3,19},{19,3},{4,20},{20... | collective-permute-start | bytes 3145736 | tf_op jit(solution)/shard_map/ppermute | solution.py:199
  374.1 65.6 %collective-permute-start.2 = (bf16[2,256,1024]{2,1,0:T(8,128)(2,1)}, bf16[2,256,1024]{2,1,0:T(8,128)(2,1)}, u32[]{:S(2)}, u32[]{:S(2)}) collective-permute-start(bf16[2,256,1024]{2,1,0:T(8,128)(2,1)} %get-tuple-element.459), channel_id=1, source_target_pairs={{0,16},{16,0},{1,17},{17,1},{2,18},{18,2},{3,19},{19,3},{4,20},{20... | collective-permute-start | bytes 3145736 | tf_op jit(solution)/shard_map/ppermute | solution.py:199
  375.7 6.7 copy-start.36
  385.0 2.6 copy-start.23
  387.4 4.6 copy-start.3
  392.0 2.0 copy-start.2
  395.6 10.7 %copy-start.7 = (bf16[2,512,8,64]{1,3,2,0:T(8,128)(2,1)S(1)}, bf16[2,512,8,64]{1,3,2,0:T(8,128)(2,1)}, u32[]{:S(2)}) copy-start(bf16[2,512,8,64]{1,3,2,0:T(8,128)(2,1)} %get-tuple-element.749) | copy-start | bytes 3145732 | tf_op jit(solution)/shard_map/while
  402.0 4.3 copy-start.4
  410.4 2.6 copy-start.23
  412.8 4.6 copy-start.3
  417.4 2.0 copy-start.2
  421.1 10.8 %copy-start.7 = (bf16[2,512,8,64]{1,3,2,0:T(8,128)(2,1)S(1)}, bf16[2,512,8,64]{1,3,2,0:T(8,128)(2,1)}, u32[]{:S(2)}) copy-start(bf16[2,512,8,64]{1,3,2,0:T(8,128)(2,1)} %get-tuple-element.749) | copy-start | bytes 3145732 | tf_op jit(solution)/shard_map/while
  427.6 4.3 copy-start.4
  439.7 6.1 copy-start.11
  439.7 6.1 copy-start.17
  441.3 34.5 %all-to-all-start.3 = ((bf16[4,2,256,512]{3,2,1,0:T(8,128)(2,1)}), bf16[4,2,256,512]{3,2,1,0:T(8,128)(2,1)}, u32[]{:S(2)}, u32[]{:S(2)}) async-start(bf16[4,2,256,512]{3,2,1,0:T(8,128)(2,1)} %copy.109), calls=%async_computation.4 | async-start | bytes 4194304 | tf_op jit(solution)/shard_map/all_to_all | solution.py:379
  445.7 32.5 %copy-start.6 = (f32[256,8,2,64]{0,3,2,1:T(8,128)S(1)}, f32[256,8,2,64]{0,3,2,1:T(8,128)}, u32[]{:S(2)}) copy-start(f32[256,8,2,64]{0,3,2,1:T(8,128)} %get-tuple-element.193) | copy-start | bytes 3145732
  445.7 32.5 %copy-start.26 = (f32[256,32]{0,1:T(8,128)S(1)}, f32[256,32]{0,1:T(8,128)}, u32[]{:S(2)}) copy-start(f32[256,32]{0,1:T(8,128)} %copy-done.25) | copy-start | bytes 98308
  445.8 32.5 %copy-start.28 = (f32[256,32]{0,1:T(8,128)S(1)}, f32[256,32]{0,1:T(8,128)}, u32[]{:S(2)}) copy-start(f32[256,32]{0,1:T(8,128)} %copy-done.27) | copy-start | bytes 98308
  445.8 93.8 %reduce-scatter.9.cloned.1.call-start = ((), (), s32[]{:S(2)}) async-start(), calls=%async_computation.13 | async-start | bytes 2228224 | tf_op jit(solution)/shard_map/reduce_scatter | solution.py:401
  477.9 138.0 %reduce-scatter.11.cloned.1.call-start = ((), (), s32[]{:S(2)}) async-start(), calls=%async_computation.14 | async-start | bytes 4456448 | tf_op jit(solution)/shard_map/reduce_scatter | solution.py:403
  478.5 7.2 copy-start.19
  478.5 7.2 copy-start.15
  478.5 7.2 copy-start.31
  490.1 134.2 %copy-start.13 = (bf16[256,1024]{1,0:T(8,128)(2,1)S(1)}, bf16[256,1024]{1,0:T(8,128)(2,1)}, u32[]{:S(2)}) copy-start(bf16[256,1024]{1,0:T(8,128)(2,1)} %multiply_convert_fusion) | copy-start | bytes 1572868
  490.1 134.2 %copy-start.34 = (f32[256]{0:T(256)S(1)}, f32[256]{0:T(256)}, u32[]{:S(2)}) copy-start(f32[256]{0:T(256)} %copy-done.33) | copy-start | bytes 3076
  490.1 134.2 %copy-start.37 = (f32[256]{0:T(256)S(1)}, f32[256]{0:T(256)}, u32[]{:S(2)}) copy-start(f32[256]{0:T(256)} %copy-done.36) | copy-start | bytes 3076
  539.6 127.7 %all-gather.10.cloned.1.call-start = ((), (), s32[]{:S(2)}) async-start(), calls=%async_computation.16 | async-start | bytes 2228224 | tf_op jit(solution)/shard_map/all_gather | solution.py:405
  539.7 5.2 collective-permute-start.5
  546.5 165.2 %all-gather.8.cloned.1.call-start = ((), (), s32[]{:S(2)}) async-start(), calls=%async_computation.15 | async-start | bytes 4456448 | tf_op jit(solution)/shard_map/all_gather | solution.py:407
  615.9 6.6 collective-permute-start.4
  624.2 3.7 copy-start.41
  624.2 3.1 copy-start.18
  624.2 3.6 copy-start.24
  627.3 2.1 copy-start.35
  630.3 14.2 %all-to-all-start.4 = ((f32[16,3,1024]{2,1,0:T(4,128)}), f32[16,3,1024]{2,1,0:T(4,128)S(1)}, u32[]{:S(2)}, u32[]{:S(2)}) async-start(f32[16,3,1024]{2,1,0:T(4,128)} %reshape.328), calls=%async_computation.6 | async-start | bytes 524288 | tf_op jit(solution)/shard_map/all_to_all | solution.py:418
  639.3 14.4 %copy-start.39 = (f32[256]{0:T(256)S(1)}, f32[256]{0:T(256)}, u32[]{:S(2)}) copy-start(f32[256]{0:T(256)} %copy-done.38) | copy-start | bytes 3076
  644.6 20.5 %copy-start.9 = (f32[256,1024]{1,0:T(8,128)S(1)}, f32[256,1024]{1,0:T(8,128)}, u32[]{:S(2)}) copy-start(f32[256,1024]{1,0:T(8,128)} %copy-done.8) | copy-start | bytes 3145732
  644.6 4.8 collective-permute-start.3
  650.2 13.6 %all-to-all-start.5 = ((f32[16,3,1024]{2,1,0:T(4,128)}), f32[16,3,1024]{2,1,0:T(4,128)S(1)}, u32[]{:S(2)}, u32[]{:S(2)}) async-start(f32[16,3,1024]{2,1,0:T(4,128)} %broadcast_in_dim.140), calls=%async_computation.7 | async-start | bytes 524288 | tf_op jit(solution)/shard_map/all_to_all | solution.py:220
  711.7 4.3 copy-start.12
  711.7 6.9 copy-start.1
  (6 other events, 5.6 us)
Sparse Core Ops, SparseCore 0:
  10.3 81.7 all-gather.11
  110.4 76.1 all-gather.5
  254.5 102.8 reduce-scatter.4
  361.3 106.8 reduce-scatter.6
  478.0 61.5 reduce-scatter.8
  544.4 71.4 reduce-scatter.10
  618.1 40.3 all-gather.9
  661.3 50.4 all-gather.7
